TPU v7x, 128 devices: a whole 4x4x4 slice. The times are simulated.
128 devices in a mesh: snap: 16 (over y, z), ord: 8 (over x, core).
Axes of the slice: x: 4, y: 4, z: 4, core: 2. Of those that a mesh axis runs over, the one named last changes fastest.
Arguments:
- images: bfloat16 [2048, 256, 1024], P(('snap', 'ord')), may hold values from -8 to 8
- cycle_masks: int32 [2048, 256], P('snap'), may hold values from 0 to 1, as said below
- weights: float32 [2048], P('snap'), may hold values from 1 to 4
- inversion: float32 [128, 128], replicated, may hold values from -1 to 2
Outputs:
- kam: float32 [128, 256, 256], P('ord', 'snap')
Inputs may be any that keep to these rules, and one draw needn't show every extreme that they name: `cycle_masks`: each entry is 0 or 1; the same 4 cycles, drawn from the seed, are 0 in every snapshot.
All inputs are finite; a program needn't handle non-finite values.
Results may differ from a plain program's by a relative error of at most 0.0015.
Values may be sent and summed in bfloat16 or wider, within the bound.
A program may use at most 64 MiB of HBM per device.

v0:
```python
import math

import jax
import jax.numpy as jnp
from jax import lax
from jax.sharding import PartitionSpec as P


def make_table(orders, angles):
    order_index = jnp.arange(orders, dtype=jnp.int32)
    angle_index = jnp.arange(angles, dtype=jnp.int32)
    phase_index = order_index[:, None] * angle_index[None, :] % angles
    radians = phase_index.astype(jnp.float32) * (2.0 * math.pi / angles)
    norming = math.sqrt(2.0 / angles)
    return jnp.concatenate(
        [jnp.cos(radians) * norming, -jnp.sin(radians) * norming], axis=0
    ).astype(jnp.bfloat16)


def weighted_gram(arrived, weight_rows):
    weighted = (arrived.astype(jnp.float32) * weight_rows[None, None, :, None]).astype(jnp.bfloat16)
    return jnp.einsum("rlsq,rlsp->lqp", weighted, arrived, preferred_element_type=jnp.float32)


def on_device(images, cycle_masks, weights, inversion):
    snap_dev, cycle_count, angles = images.shape
    orders = inversion.shape[0]
    ord_index = lax.axis_index("ord")
    dft_table = make_table(orders, angles)
    group_masks = cycle_masks.astype(jnp.float32)
    own_masks = lax.dynamic_slice_in_dim(group_masks, ord_index * snap_dev, snap_dev, 0)
    coeffs = jnp.einsum("ka,sqa->ksq", dft_table, images, preferred_element_type=jnp.float32)
    coeffs = (
        (coeffs * own_masks[None]).astype(jnp.bfloat16).reshape(2, orders, snap_dev, cycle_count)
    )
    masked_weight = group_masks * weights[:, None]
    partial_count = jnp.einsum(
        "sq,sp->qp", masked_weight, group_masks, precision=lax.Precision.HIGHEST
    )
    arrived = lax.all_to_all(coeffs, "ord", split_axis=1, concat_axis=2, tiled=True)
    partial_value = weighted_gram(arrived, weights)
    gram_sum, pair_count = (
        lax.psum_scatter(partial_value, "snap", scatter_dimension=1, tiled=True),
        lax.psum_scatter(partial_count[None], "snap", scatter_dimension=1, tiled=True),
    )
    pair_count = pair_count[0]
    correl = gram_sum / jnp.maximum(pair_count, 1.0)[None]
    local_orders = correl.shape[0]
    own_rows = lax.dynamic_slice_in_dim(inversion, ord_index * local_orders, local_orders, 0)
    return jnp.einsum(
        "ln,nqp->lqp",
        own_rows,
        lax.all_gather(correl, "ord", axis=0, tiled=True),
        precision=lax.Precision.HIGHEST,
    )


def solution(mesh):
    placed = (P(("snap", "ord"), None, None), P("snap", None), P("snap"), P())
    return jax.shard_map(
        on_device, mesh=mesh, in_specs=placed, out_specs=P("ord", "snap", None), check_vma=False
    )
```

profile of v0, /device:TPU:1, one launch (start us, length us, event | category | flops | bytes accessed | tf_op | source)
XLA Modules:
  0.0 220.8 jit_solution(15306926663865031668)
XLA Ops:
  6.5 0.0 copy-start
  6.5 2.2 multiply_convert_fusion.5
  8.7 0.9 convert_element_type.19
  9.7 5.8 %multiply_convert_fusion.1 = bf16[256,16,256]{2,0,1:T(8,128)(2,1)S(1)} fusion(bf16[16,256,1024]{2,1,0:T(8,128)(2,1)} %param.4, f32[16,256]{1,0:T(8,128)S(1)} %constant_dynamic-slice_fusion, bf16[128,1024]{1,0:T(8,128)(2,1)S(1)} %get-tuple-element.5, bf16[128,1024]{1,0:T(8,128)(2,1)S(1)} %get-tuple-element.6), kind=kOutput, calls=%fused_computation.1 | convolution fusion | flops 2150629376 | bytes 11026432 | tf_op jit(solution)/shard_map/ka,sqa->ksq/dot_general | solution.py:32
  15.4 2.5 %copy.12 = bf16[2,128,16,256]{3,2,0,1:T(8,128)(2,1)} copy(bf16[2,128,16,256]{3,1,0,2:T(8,128)(2,1)S(1)} %bitcast.21) | data formatting | bytes 4194304 | tf_op jit(solution)/shard_map/reshape | solution.py:34
  18.0 0.0 copy-start.1
  18.0 0.0 copy-start.2
  18.0 5.9 %all-to-all-start = ((bf16[2,128,16,256]{3,2,0,1:T(8,128)(2,1)}), bf16[2,128,16,256]{3,2,0,1:T(8,128)(2,1)S(1)}, u32[]{:S(2)}, u32[]{:S(2)}) async-start(bf16[2,128,16,256]{3,2,0,1:T(8,128)(2,1)} %copy.12), calls=%async_computation | async-start | bytes 4194304 | tf_op jit(solution)/shard_map/all_to_all | solution.py:40
  23.9 0.0 reduce-scatter.5.cloned.1.call-start
  23.9 0.0 copy-done.1
  23.9 0.0 copy-done.2
  23.9 1.2 convolution_bitcast_fusion
  25.1 0.0 reduce-scatter.5.cloned.1.call-update
  25.1 0.0 reduce-scatter.3.cloned.1.call-start
  25.2 25.1 %all-to-all-done = bf16[2,128,16,256]{3,2,0,1:T(8,128)(2,1)S(1)} async-done(((bf16[2,128,16,256]{3,2,0,1:T(8,128)(2,1)}), bf16[2,128,16,256]{3,2,0,1:T(8,128)(2,1)S(1)}, u32[]{:S(2)}, u32[]{:S(2)}) %all-to-all-start) | async-done | bytes 2097184 | tf_op jit(solution)/shard_map/all_to_all | solution.py:40
  50.2 0.2 copy.14
  50.5 3.0 %fusion.1 = f32[16,256,256]{2,1,0:T(8,128)} fusion(bf16[2,16,128,256]{3,2,1,0:T(8,128)(2,1)S(1)} %bitcast.19, f32[128]{0:T(128)S(1)} %copy-done.2), kind=kOutput, calls=%fused_computation.3 | convolution fusion | flops 540016640 | bytes 6291968 | tf_op jit(solution)/shard_map/rlsq,rlsp->lqp/dot_general | solution.py:22
  53.5 0.0 reduce-scatter.3.cloned.1.call-update
  53.5 0.0 all-gather.2.cloned.1.call-start
  53.5 47.1 %reduce-scatter.5.cloned.1.call-done = f32[1,16,256]{2,1,0:T(8,128)} async-done(((f32[1,256,256]{2,1,0:T(8,128)}), f32[1,16,256]{2,1,0:T(8,128)}) %reduce-scatter.5.cloned.1.call-update) | async-done | bytes 16400 | tf_op jit(solution)/shard_map/reduce_scatter | solution.py:44
  100.7 0.7 maximum_bitcast_fusion.2
  101.4 80.1 %reduce-scatter.3.cloned.1.call-done = f32[16,16,256]{2,1,0:T(8,128)} async-done(((f32[16,256,256]{2,1,0:T(8,128)}), f32[16,16,256]{2,1,0:T(8,128)}) %reduce-scatter.3.cloned.1.call-update) | async-done | bytes 262160 | tf_op jit(solution)/shard_map/reduce_scatter | solution.py:43
  181.5 1.7 broadcast_divide_fusion
  183.2 0.0 all-gather.2.cloned.1.call-update
  183.2 26.5 %all-gather.2.cloned.1.call-done = f32[128,16,256]{2,1,0:T(8,128)} async-done(((f32[16,16,256]{2,1,0:T(8,128)}), f32[128,16,256]{2,1,0:T(8,128)}) %all-gather.2.cloned.1.call-update) | async-done | bytes 2097168 | tf_op jit(solution)/shard_map/all_gather | solution.py:53
  209.7 0.0 copy-done
  209.7 3.8 %fusion.2 = f32[16,16,256]{2,0,1:T(8,128)S(1)} fusion(f32[128,16,256]{2,1,0:T(8,128)} %all-gather.2.cloned.1.call-done, f32[128,128]{1,0:T(8,128)S(1)} %copy-done, s32[]{:T(128)S(6)} %select_n.13), kind=kOutput, calls=%fused_computation.4 | convolution fusion | flops 100663296 | bytes 2367492 | tf_op jit(solution)/shard_map/ln,nqp->lqp/dot_general | solution.py:50
  213.5 0.9 copy.17
  (1 shorter events, 0.0 us)
Async XLA Ops:
  6.5 203.2 %copy-start = (f32[128,128]{1,0:T(8,128)S(1)}, f32[128,128]{1,0:T(8,128)}, u32[]{:S(2)}) copy-start(f32[128,128]{1,0:T(8,128)} %param.7) | copy-start | bytes 196612
  18.0 5.9 %copy-start.1 = (s32[128,256]{1,0:T(8,128)S(1)}, s32[128,256]{1,0:T(8,128)}, u32[]{:S(2)}) copy-start(s32[128,256]{1,0:T(8,128)} %param.5) | copy-start | bytes 393220
  18.0 5.9 %copy-start.2 = (f32[128]{0:T(128)S(1)}, f32[128]{0:T(128)}, u32[]{:S(2)}) copy-start(f32[128]{0:T(128)} %param.6) | copy-start | bytes 1540
  18.0 32.3 %all-to-all-start = ((bf16[2,128,16,256]{3,2,0,1:T(8,128)(2,1)}), bf16[2,128,16,256]{3,2,0,1:T(8,128)(2,1)S(1)}, u32[]{:S(2)}, u32[]{:S(2)}) async-start(bf16[2,128,16,256]{3,2,0,1:T(8,128)(2,1)} %copy.12), calls=%async_computation | async-start | bytes 4194304 | tf_op jit(solution)/shard_map/all_to_all | solution.py:40
  23.9 76.8 %reduce-scatter.5.cloned.1.call-start = ((), (), s32[]{:S(2)}) async-start(), calls=%async_computation.4 | async-start | bytes 278528 | tf_op jit(solution)/shard_map/reduce_scatter | solution.py:44
  25.1 156.3 %reduce-scatter.3.cloned.1.call-start = ((), (), s32[]{:S(2)}) async-start(), calls=%async_computation.3 | async-start | bytes 4456448 | tf_op jit(solution)/shard_map/reduce_scatter | solution.py:43
  53.5 156.2 %all-gather.2.cloned.1.call-start = ((), (), s32[]{:S(2)}) async-start(), calls=%async_computation.5 | async-start | bytes 2359296 | tf_op jit(solution)/shard_map/all_gather | solution.py:53
Sparse Core Ops, SparseCore 0:
  27.9 72.7 reduce-scatter.4
  104.4 77.0 reduce-scatter.2
  183.3 26.3 all-gather.1
where the time goes:
time: 221 us
  waiting for transfers between devices  179 us (81%)
  matrix products  13.7 us (6%)
  between operations  13.2 us (6%)
  starting transfers between devices  6.02 us (3%)
  other arithmetic  5.5 us (2%)
  local copies, waits for them, and re-layouts  3.64 us (2%)
    reduce_scatter x1, waiting for transfers between devices, on_device(): lax.psum_scatter(partial_value, 'snap', scatter_dimension=1, tiled=True)  80.1 us
    reduce_scatter x1, waiting for transfers between devices, on_device(): lax.psum_scatter(partial_count[None], 'snap', scatter_dimension=1, tiled=...  47.1 us
    all_gather x1, waiting for transfers between devices, on_device(): lax.all_gather(correl, 'ord', axis=0, tiled=True)  26.5 us
    all_to_all x1, waiting for transfers between devices, on_device(): lax.all_to_all(coeffs, 'ord', split_axis=1, concat_axis=2, tiled=True)  25.1 us
    all_to_all x1, starting transfers between devices, on_device(): lax.all_to_all(coeffs, 'ord', split_axis=1, concat_axis=2, tiled=True)  5.93 us
    dot_general x1, matrix products, on_device(): jnp.einsum('ka,sqa->ksq', dft_table, images, preferred_element_type=jnp.f...  5.76 us
  transfers between devices with their start and end apart: 4, of which 4 were waited for; matrix products, arithmetic and copies ran while one was open for 2% of the time, Pallas kernels for 0%

commit v1 on v0

v1 whole, which is shorter than its diff:
```python
import functools
import math

import jax
import jax.numpy as jnp
import numpy as np
from jax import lax
from jax.experimental import pallas as pl
from jax.experimental.pallas import tpu as pltpu
from jax.sharding import PartitionSpec as P

MESH = pl.DeviceIdType.MESH
SIDE = 4
GROUPS = SIDE * SIDE
LINE = 2 * SIDE
SNAPS = 16
CYCLES = 256
ANGLES = 1024
ORDERS = 128
HALF = ORDERS // 2


def make_table():
    order_index = np.arange(ORDERS)
    angle_index = np.arange(ANGLES)
    phase_index = order_index[:, None] * angle_index[None, :] % ANGLES
    radians = phase_index.astype(np.float32) * np.float32(2.0 * math.pi / ANGLES)
    norming = np.float32(math.sqrt(2.0 / ANGLES))
    table = np.concatenate([np.cos(radians) * norming, -np.sin(radians) * norming], axis=0)
    return table.astype(jnp.bfloat16)


def slot_offsets(slot):
    dy = slot % SIDE
    dz = (dy + slot // SIDE) % SIDE
    return dy, dz


def kernel(
    img_hbm, msk_hbm, wts_hbm, inv_hbm, tab_hbm, out_ref,
    img, tab, msk, wts, inv, spectra, coeffs, arrived, notes, notices, gram, tiles, kams,
    in_sems, img_sems, a_send, a_recv, n_send, n_recv, g_send, g_recv, h_send, h_recv, k_send, k_recv, ready,
):
    s = lax.axis_index("snap")
    o = lax.axis_index("ord")
    y, z = s // SIDE, s % SIDE
    x, c = o // 2, o % 2
    x_row, x_lane = x // 2, x % 2

    def group_at(dy, dz):
        return ((y + dy) % SIDE) * SIDE + (z + dz) % SIDE

    for k in range(SNAPS):
        pltpu.make_async_copy(img_hbm.at[k], img.at[k], img_sems.at[k]).start()
    small = [
        pltpu.make_async_copy(src, dst, in_sems.at[k])
        for k, (src, dst) in enumerate(
            [(tab_hbm, tab), (msk_hbm, msk), (wts_hbm, wts), (inv_hbm, inv)]
        )
    ]
    for copy in small:
        copy.start()

    barrier = pltpu.get_barrier_semaphore()

    def greet_line(k, carry):
        pl.semaphore_signal(barrier, inc=1, device_id=(s, (o + k) % LINE), device_id_type=MESH)
        return carry

    def greet_groups(k, carry):
        pl.semaphore_signal(barrier, inc=1, device_id=((s + k) % GROUPS, o), device_id_type=MESH)
        return carry

    lax.fori_loop(1, LINE, greet_line, 0)
    lax.fori_loop(1, GROUPS, greet_groups, 0)

    for copy in small[1:]:
        copy.wait()
    mask = msk[...].astype(jnp.float32)
    mask_half = msk[:, pl.ds(pl.multiple_of(x_lane * 128, 128), 128)].astype(jnp.float32)
    gram[:, 0:128] = jnp.dot(
        mask.T * wts[...], mask_half,
        precision=lax.Precision.HIGHEST, preferred_element_type=jnp.float32,
    )
    weight_rows = jnp.broadcast_to(wts[...], (8, 128))
    for k in range(GROUPS):
        notes[k, 0:8, :] = gram[pl.ds(pl.multiple_of(16 * k + 8 * x_row, 8), 8), 0:128]
        notes[k, 8:16, :] = weight_rows
    notices[0] = notes[s]

    pl.semaphore_wait(barrier, LINE - 1 + GROUPS - 1)

    def tell(k, carry):
        pl.semaphore_signal(ready, inc=1, device_id=((s + k) % GROUPS, o), device_id_type=MESH)
        return carry

    lax.fori_loop(1, GROUPS, tell, 0)

    def send_note(slot, carry):
        group = group_at(*slot_offsets(slot))
        pltpu.make_async_remote_copy(
            notes.at[group], notices.at[slot], n_send, n_recv, device_id=(group, o), device_id_type=MESH
        ).start()
        return carry

    lax.fori_loop(1, GROUPS, send_note, 0)

    small[0].wait()

    def transform(k, carry):
        pltpu.make_async_copy(img_hbm.at[k], img.at[k], img_sems.at[k]).wait()
        product = lax.dot_general(
            tab[...], img[k], (((1,), (1,)), ((), ())), preferred_element_type=jnp.float32
        )
        row = msk[pl.ds(o * SNAPS + k, 1), :].astype(jnp.float32)
        product = product * row
        place = pl.multiple_of(k * 2 * ORDERS, 2 * ORDERS)
        for lane in range(2):
            spectra[lane, pl.ds(place, 2 * ORDERS), :] = product[:, 128 * lane : 128 * lane + 128]
        return carry

    lax.fori_loop(0, SNAPS, transform, 0)

    pl.semaphore_wait(ready, GROUPS - 1)

    def gather(order):
        for part in range(2):
            for lane in range(2):
                rows = spectra[lane, pl.ds(part * ORDERS + order, SNAPS, stride=2 * ORDERS), :]
                coeffs[order, part, :, 128 * lane : 128 * lane + 128] = rows.astype(jnp.bfloat16)

    own_order = c * HALF + x * GROUPS + s
    gather(own_order)
    pltpu.make_async_copy(coeffs.at[own_order], arrived.at[0, :, o], a_recv.at[0]).start()

    def send_coeffs(i, carry):
        wave, step = i // 32, i % 32
        dy = step % 4
        dz = (dy + wave) % 4
        dx = (step // 4) % 4
        dc = step // 16
        group = group_at(dy, dz)
        there_x, there_c = (x + dx) % SIDE, (c + dc) % 2
        order = there_c * HALF + there_x * GROUPS + group
        gather(order)
        slot = wave * 4 + dy
        pltpu.make_async_remote_copy(
            coeffs.at[order], arrived.at[slot, :, o], a_send, a_recv.at[slot],
            device_id=(group, there_x * 2 + there_c), device_id_type=MESH,
        ).start()
        return carry

    lax.fori_loop(1, ORDERS, send_coeffs, 0)

    pltpu.make_async_copy(notices.at[pl.ds(1, 15)], notices.at[pl.ds(1, 15)], n_recv).wait()
    gram[...] = jnp.zeros_like(gram)

    def add_group(slot, carry):
        pltpu.make_async_copy(arrived.at[slot], arrived.at[slot], a_recv.at[slot]).wait()
        block = arrived[slot].reshape(2 * LINE * SNAPS, CYCLES)
        weight = notices[slot, 8:9, :]
        weight = jnp.concatenate([weight, weight], axis=1)
        weighted = (block.astype(jnp.float32).T * weight).astype(jnp.bfloat16)
        gram[...] += jnp.dot(weighted, block, preferred_element_type=jnp.float32)
        return carry

    lax.fori_loop(0, GROUPS, add_group, 0)

    tile_rows = pl.ds(pl.multiple_of(8 * own_order, 8), 8)

    def gram_tile(group, chip):
        row = pl.multiple_of(16 * group + 8 * (chip // 2), 8)
        lane = pl.multiple_of(128 * (chip % 2), 128)
        return gram.at[pl.ds(row, 8), pl.ds(lane, 128)]

    pltpu.make_async_copy(gram_tile(s, x), tiles.at[tile_rows], g_recv).start()

    def send_tile(i, carry):
        wave, step = i // 16, i % 16
        dy = step % 4
        dz = (dy + wave) % 4
        dx = step // 4
        group = group_at(dy, dz)
        there_x = (x + dx) % SIDE
        pltpu.make_async_remote_copy(
            gram_tile(group, there_x), tiles.at[tile_rows], g_send, g_recv,
            device_id=(group, there_x * 2 + c), device_id_type=MESH,
        ).start()
        return carry

    lax.fori_loop(1, HALF, send_tile, 0)

    own_half = tiles.at[pl.ds(pl.multiple_of(8 * HALF * c, 8 * HALF), 8 * HALF)]
    pltpu.make_async_copy(own_half, own_half, g_recv).wait()
    swap = pltpu.make_async_remote_copy(
        own_half, own_half, h_send, h_recv, device_id=(s, x * 2 + 1 - c), device_id_type=MESH
    )
    swap.start()
    count = notices[0, 0:8, :]
    for k in range(1, GROUPS):
        count += notices[k, 0:8, :]
    count = jnp.maximum(count, 1.0)
    own_inv = jnp.concatenate(
        [inv[pl.ds(pl.multiple_of(32 * k + 16 * c, 16), 16), :] for k in range(SIDE)], axis=0
    )
    swap.wait()

    flat_kams = kams.reshape(HALF * 8, 128)
    for r in range(8):
        grams = tiles[pl.ds(r, ORDERS, stride=8), :]
        correl = grams / count[r : r + 1, :]
        flat_kams[pl.ds(r, HALF, stride=8), :] = jnp.dot(
            own_inv, correl, precision=lax.Precision.HIGHEST, preferred_element_type=jnp.float32
        )

    place = out_ref.at[:, pl.ds(pl.multiple_of(8 * x_row, 8), 8), pl.ds(pl.multiple_of(128 * x_lane, 128), 128)]
    for d in range(1, SIDE):
        there_x = (x + d) % SIDE
        pltpu.make_async_remote_copy(
            kams.at[pl.ds(16 * there_x, 16)], place, k_send, k_recv,
            device_id=(s, there_x * 2 + c), device_id_type=MESH,
        ).start()
    pltpu.make_async_copy(kams.at[pl.ds(16 * x, 16)], place, k_recv).start()

    pltpu.make_async_copy(notes.at[pl.ds(0, 15)], notes.at[pl.ds(0, 15)], n_send).wait()
    pltpu.make_async_copy(coeffs.at[pl.ds(0, 127)], coeffs.at[pl.ds(0, 127)], a_send).wait()
    pltpu.make_async_copy(tiles.at[pl.ds(0, 504)], tiles.at[pl.ds(0, 504)], g_send).wait()
    pltpu.make_async_copy(kams.at[pl.ds(0, 48)], kams.at[pl.ds(0, 48)], k_send).wait()
    pltpu.make_async_copy(out_ref, out_ref, k_recv).wait()


def on_device(images, cycle_masks, weights, inversion):
    hbm = pl.BlockSpec(memory_space=pl.ANY)
    dma, regular = pltpu.SemaphoreType.DMA, pltpu.SemaphoreType.REGULAR
    f32, bf16 = jnp.float32, jnp.bfloat16
    return pl.pallas_call(
        kernel,
        out_shape=jax.ShapeDtypeStruct((16, 16, CYCLES), f32),
        in_specs=[hbm] * 5,
        out_specs=hbm,
        scratch_shapes=[
            pltpu.VMEM((SNAPS, CYCLES, ANGLES), bf16),
            pltpu.VMEM((2 * ORDERS, ANGLES), bf16),
            pltpu.VMEM((LINE * SNAPS, CYCLES), jnp.int32),
            pltpu.VMEM((1, LINE * SNAPS), f32),
            pltpu.VMEM((ORDERS, ORDERS), f32),
            pltpu.VMEM((2, SNAPS * 2 * ORDERS, 128), f32),
            pltpu.VMEM((ORDERS, 2, SNAPS, CYCLES), bf16),
            pltpu.VMEM((GROUPS, 2, LINE, SNAPS, CYCLES), bf16),
            pltpu.VMEM((GROUPS, 16, 128), f32),
            pltpu.VMEM((GROUPS, 16, 128), f32),
            pltpu.VMEM((CYCLES, CYCLES), f32),
            pltpu.VMEM((ORDERS * 8, 128), f32),
            pltpu.VMEM((HALF, 8, 128), f32),
            dma((4,)),
            dma((SNAPS,)),
            dma,
            dma((GROUPS,)),
            dma, dma, dma, dma, dma, dma, dma, dma,
            regular,
        ],
        compiler_params=pltpu.CompilerParams(
            collective_id=0, has_side_effects=True, vmem_limit_bytes=48 * 2**20
        ),
        name="kam",
    )(images, cycle_masks, weights.reshape(1, -1), inversion, jnp.asarray(make_table()))


def solution(mesh):
    placed = (P(("snap", "ord"), None, None), P("snap", None), P("snap"), P())
    return jax.shard_map(
        on_device, mesh=mesh, in_specs=placed, out_specs=P("ord", "snap", None), check_vma=False
    )
```

time: 221 us -> 62.3 us (0.28)
  waiting for transfers between devices: 179 us -> 0 us
  Pallas kernels: 0 us -> 58 us
  matrix products: 13.7 us -> 0 us
  between operations: 13.2 us -> 0.01 us
  starting transfers between devices: 6.02 us -> 0 us
  other arithmetic: 5.5 us -> 0 us
    reduce_scatter x2 -> x0, waiting for transfers between devices: 127 us -> none  [the longest x1 80.1 us: on_device(): lax.psum_scatter(partial_value, 'snap', scatter_dimension=1, tiled=True)]
    pallas_call x0 -> x1, Pallas kernels: none -> 58 us  [on_device(): pl.pallas_call(kernel, out_shape=jax.ShapeDtypeStruct((16, 16, CYCLES), f...]
    all_gather x1 -> x0, waiting for transfers between devices: 26.5 us -> none  [on_device(): lax.all_gather(correl, 'ord', axis=0, tiled=True)]
    all_to_all x1 -> x0, waiting for transfers between devices: 25.1 us -> none  [on_device(): lax.all_to_all(coeffs, 'ord', split_axis=1, concat_axis=2, tiled=True)]
    dot_general x4 -> x0, matrix products: 13.7 us -> none  [the longest x1 5.76 us: on_device(): jnp.einsum('ka,sqa->ksq', dft_table, images, preferred_element_type=jnp.f...]
    all_to_all x1 -> x0, starting transfers between devices: 5.93 us -> none  [on_device(): lax.all_to_all(coeffs, 'ord', split_axis=1, concat_axis=2, tiled=True)]
    unnamed x6 -> x9, local copies, waits for them, and re-layouts: 0.01 us -> 4.14 us
    reshape x1 -> x0, local copies, waits for them, and re-layouts: 2.53 us -> none  [on_device(): (coeffs * own_masks[None]).astype(jnp.bfloat16)]
  transfers between devices with their start and end apart: 4 -> 0, of which waited for: 4 -> 0; matrix products, arithmetic and copies ran while one was open for 2% -> 0% of each run, Pallas kernels for 0% -> 0%
where the time goes in v1:
time: 62.3 us; the launch traced here: 62.1 us
  Pallas kernels  58 us (93%)
  local copies, waits for them, and re-layouts  4.14 us (7%)
    pallas_call x1, Pallas kernels, on_device(): pl.pallas_call(kernel, out_shape=jax.ShapeDtypeStruct((16, 16, CYCLES), f...  58 us
    unnamed x9, local copies, waits for them, and re-layouts  4.14 us

profile of v1, /device:TPU:1, one launch (start us, length us, event | category | flops | bytes accessed | tf_op | source)
XLA Modules:
  0.0 62.1 jit_solution(6806213941452957355)
XLA Ops:
  0.0 0.0 copy-start
  0.0 1.0 %copy-done = bf16[256,1024]{1,0:T(8,128)(2,1)S(1)} copy-done((bf16[256,1024]{1,0:T(8,128)(2,1)S(1)}, bf16[256,1024]{1,0:T(8,128)(2,1)}, u32[]{:S(2)}) %copy-start) | copy-done | bytes 524312
  1.0 0.0 copy-start.1
  1.0 0.9 %copy-done.1 = s32[128,256]{1,0:T(8,128)S(1)} copy-done((s32[128,256]{1,0:T(8,128)S(1)}, s32[128,256]{1,0:T(8,128)}, u32[]{:S(2)}) %copy-start.1) | copy-done | bytes 131096
  1.9 0.0 copy-start.2
  1.9 0.8 %copy-done.2 = f32[128,128]{1,0:T(8,128)S(1)} copy-done((f32[128,128]{1,0:T(8,128)S(1)}, f32[128,128]{1,0:T(8,128)}, u32[]{:S(2)}) %copy-start.2) | copy-done | bytes 65560
  2.8 0.0 copy-start.3
  2.8 0.7 %copy-done.3 = f32[128]{0:T(128)S(1)} copy-done((f32[128]{0:T(128)S(1)}, f32[128]{0:T(128)}, u32[]{:S(2)}) %copy-start.3) | copy-done | bytes 536
  3.4 58.0 %kam.1 = f32[16,16,256]{2,1,0:T(8,128)S(1)} custom-call(bf16[16,256,1024]{2,1,0:T(8,128)(2,1)} %img_hbm.1, s32[128,256]{1,0:T(8,128)S(1)} %copy-done.1, f32[1,128]{1,0:T(1,128)S(1)} %bitcast.1, f32[128,128]{1,0:T(8,128)S(1)} %copy-done.2, bf16[256,1024]{1,0:T(8,128)(2,1)S(1)} %copy-done), custom_call_target="tpu_custom_call" | custom-call | tf_op jit(solution)/shard_map/kam/pallas_call | solution.py:236
  61.4 0.7 %copy.7 = f32[16,16,256]{2,1,0:T(8,128)} copy(f32[16,16,256]{2,1,0:T(8,128)S(1)} %kam.1) | data formatting | bytes 524288
Async XLA Ops:
  0.0 1.0 %copy-start = (bf16[256,1024]{1,0:T(8,128)(2,1)S(1)}, bf16[256,1024]{1,0:T(8,128)(2,1)}, u32[]{:S(2)}) copy-start(bf16[256,1024]{1,0:T(8,128)(2,1)} %constant.2.clone.tab_hbm) | copy-start | bytes 1572868
  1.0 0.9 %copy-start.1 = (s32[128,256]{1,0:T(8,128)S(1)}, s32[128,256]{1,0:T(8,128)}, u32[]{:S(2)}) copy-start(s32[128,256]{1,0:T(8,128)} %msk_hbm.1) | copy-start | bytes 393220
  1.9 0.8 %copy-start.2 = (f32[128,128]{1,0:T(8,128)S(1)}, f32[128,128]{1,0:T(8,128)}, u32[]{:S(2)}) copy-start(f32[128,128]{1,0:T(8,128)} %inv_hbm.1) | copy-start | bytes 196612
  2.8 0.7 %copy-start.3 = (f32[128]{0:T(128)S(1)}, f32[128]{0:T(128)}, u32[]{:S(2)}) copy-start(f32[128]{0:T(128)} %param.7) | copy-start | bytes 1540

commit v2 on v1

--- a/solution.py
+++ b/solution.py
@@ -18,6 +18,7 @@
 ANGLES = 1024
 ORDERS = 128
 HALF = ORDERS // 2
+CHUNK = 4
 
 
 def make_table():
@@ -34,6 +35,10 @@
     dy = slot % SIDE
     dz = (dy + slot // SIDE) % SIDE
     return dy, dz
+
+
+def farthest_first(k):
+    return jnp.where(k == 3, 0, jnp.where(k == 2, 3, 2 - k))
 
 
 def kernel(
@@ -50,16 +55,19 @@
     def group_at(dy, dz):
         return ((y + dy) % SIDE) * SIDE + (z + dz) % SIDE
 
-    for k in range(SNAPS):
-        pltpu.make_async_copy(img_hbm.at[k], img.at[k], img_sems.at[k]).start()
     small = [
         pltpu.make_async_copy(src, dst, in_sems.at[k])
         for k, (src, dst) in enumerate(
             [(tab_hbm, tab), (msk_hbm, msk), (wts_hbm, wts), (inv_hbm, inv)]
         )
     ]
-    for copy in small:
-        copy.start()
+    small[0].start()
+    for k in range(SNAPS // CHUNK):
+        part = pl.ds(k * CHUNK, CHUNK)
+        pltpu.make_async_copy(img_hbm.at[part], img.at[part], img_sems.at[k]).start()
+        if k == 0:
+            for copy in small[1:]:
+                copy.start()
 
     barrier = pltpu.get_barrier_semaphore()
 
@@ -107,19 +115,22 @@
 
     small[0].wait()
 
-    def transform(k, carry):
-        pltpu.make_async_copy(img_hbm.at[k], img.at[k], img_sems.at[k]).wait()
-        product = lax.dot_general(
-            tab[...], img[k], (((1,), (1,)), ((), ())), preferred_element_type=jnp.float32
-        )
-        row = msk[pl.ds(o * SNAPS + k, 1), :].astype(jnp.float32)
-        product = product * row
-        place = pl.multiple_of(k * 2 * ORDERS, 2 * ORDERS)
-        for lane in range(2):
-            spectra[lane, pl.ds(place, 2 * ORDERS), :] = product[:, 128 * lane : 128 * lane + 128]
-        return carry
-
-    lax.fori_loop(0, SNAPS, transform, 0)
+    def transform(chunk, carry):
+        first = chunk * CHUNK
+        loads = img.at[pl.ds(first, CHUNK)]
+        pltpu.make_async_copy(loads, loads, img_sems.at[chunk]).wait()
+        for u in range(CHUNK):
+            k = first + u
+            product = lax.dot_general(
+                tab[...], img[k], (((1,), (1,)), ((), ())), preferred_element_type=jnp.float32
+            )
+            product = product * msk[pl.ds(o * SNAPS + k, 1), :].astype(jnp.float32)
+            place = pl.multiple_of(k * 2 * ORDERS, 2 * ORDERS)
+            for lane in range(2):
+                spectra[lane, pl.ds(place, 2 * ORDERS), :] = product[:, 128 * lane : 128 * lane + 128]
+        return carry
+
+    lax.fori_loop(0, SNAPS // CHUNK, transform, 0)
 
     pl.semaphore_wait(ready, GROUPS - 1)
 
@@ -173,29 +184,36 @@
         lane = pl.multiple_of(128 * (chip % 2), 128)
         return gram.at[pl.ds(row, 8), pl.ds(lane, 128)]
 
-    pltpu.make_async_copy(gram_tile(s, x), tiles.at[tile_rows], g_recv).start()
+    pltpu.make_async_copy(gram_tile(s, x), tiles.at[tile_rows], g_recv.at[0]).start()
 
     def send_tile(i, carry):
         wave, step = i // 16, i % 16
-        dy = step % 4
-        dz = (dy + wave) % 4
-        dx = step // 4
+        dx = farthest_first(wave)
+        dy = farthest_first(step % 4)
+        dz = farthest_first(step // 4)
         group = group_at(dy, dz)
         there_x = (x + dx) % SIDE
-        pltpu.make_async_remote_copy(
-            gram_tile(group, there_x), tiles.at[tile_rows], g_send, g_recv,
-            device_id=(group, there_x * 2 + c), device_id_type=MESH,
-        ).start()
-        return carry
-
-    lax.fori_loop(1, HALF, send_tile, 0)
-
-    own_half = tiles.at[pl.ds(pl.multiple_of(8 * HALF * c, 8 * HALF), 8 * HALF)]
-    pltpu.make_async_copy(own_half, own_half, g_recv).wait()
-    swap = pltpu.make_async_remote_copy(
-        own_half, own_half, h_send, h_recv, device_id=(s, x * 2 + 1 - c), device_id_type=MESH
-    )
-    swap.start()
+
+        @pl.when(i < HALF - 1)
+        def _():
+            pltpu.make_async_remote_copy(
+                gram_tile(group, there_x), tiles.at[tile_rows], g_send, g_recv.at[dx],
+                device_id=(group, there_x * 2 + c), device_id_type=MESH,
+            ).start()
+
+        return carry
+
+    lax.fori_loop(0, HALF, send_tile, 0)
+
+    for wave in range(SIDE):
+        dx = (2, 1, 3, 0)[wave]
+        row = pl.multiple_of(8 * (c * HALF + ((x + SIDE - dx) % SIDE) * GROUPS), 8 * GROUPS)
+        part = tiles.at[pl.ds(row, 8 * GROUPS)]
+        pltpu.make_async_copy(part, part, g_recv.at[dx]).wait()
+        swap = pltpu.make_async_remote_copy(
+            part, part, h_send, h_recv, device_id=(s, x * 2 + 1 - c), device_id_type=MESH
+        )
+        swap.start()
     count = notices[0, 0:8, :]
     for k in range(1, GROUPS):
         count += notices[k, 0:8, :]
@@ -203,7 +221,10 @@
     own_inv = jnp.concatenate(
         [inv[pl.ds(pl.multiple_of(32 * k + 16 * c, 16), 16), :] for k in range(SIDE)], axis=0
     )
-    swap.wait()
+    own_half = tiles.at[pl.ds(pl.multiple_of(8 * HALF * c, 8 * HALF), 8 * HALF)]
+    other_half = tiles.at[pl.ds(pl.multiple_of(8 * HALF * (1 - c), 8 * HALF), 8 * HALF)]
+    pltpu.make_async_copy(own_half, own_half, h_send).wait()
+    pltpu.make_async_copy(other_half, other_half, h_recv).wait()
 
     flat_kams = kams.reshape(HALF * 8, 128)
     for r in range(8):
@@ -230,14 +251,14 @@
 
 
 def on_device(images, cycle_masks, weights, inversion):
-    hbm = pl.BlockSpec(memory_space=pl.ANY)
+    operands = (images, cycle_masks, weights.reshape(1, -1), inversion, jnp.asarray(make_table()))
     dma, regular = pltpu.SemaphoreType.DMA, pltpu.SemaphoreType.REGULAR
     f32, bf16 = jnp.float32, jnp.bfloat16
     return pl.pallas_call(
         kernel,
-        out_shape=jax.ShapeDtypeStruct((16, 16, CYCLES), f32),
-        in_specs=[hbm] * 5,
-        out_specs=hbm,
+        out_shape=pltpu.VMEM((16, 16, CYCLES), f32),
+        in_specs=[pl.BlockSpec(memory_space=pltpu.HBM)] * 5,
+        out_specs=pl.BlockSpec(memory_space=pltpu.VMEM),
         scratch_shapes=[
             pltpu.VMEM((SNAPS, CYCLES, ANGLES), bf16),
             pltpu.VMEM((2 * ORDERS, ANGLES), bf16),
@@ -253,17 +274,19 @@
             pltpu.VMEM((ORDERS * 8, 128), f32),
             pltpu.VMEM((HALF, 8, 128), f32),
             dma((4,)),
-            dma((SNAPS,)),
+            dma((SNAPS // CHUNK,)),
             dma,
             dma((GROUPS,)),
-            dma, dma, dma, dma, dma, dma, dma, dma,
+            dma, dma, dma,
+            dma((SIDE,)),
+            dma, dma, dma, dma,
             regular,
         ],
         compiler_params=pltpu.CompilerParams(
             collective_id=0, has_side_effects=True, vmem_limit_bytes=48 * 2**20
         ),
         name="kam",
-    )(images, cycle_masks, weights.reshape(1, -1), inversion, jnp.asarray(make_table()))
+    )(*(pltpu.with_memory_space_constraint(value, pltpu.HBM) for value in operands))
 
 
 def solution(mesh):

time: 62.3 us -> 55.3 us (0.89)
  Pallas kernels: 58 us -> 54.5 us
  local copies, waits for them, and re-layouts: 4.14 us -> 0.71 us
    pallas_call x1, Pallas kernels: 58 us -> 54.5 us  [on_device(): pl.pallas_call(kernel, out_shape=pltpu.VMEM((16, 16, CYCLES), f32), in_sp...]
    unnamed x9 -> x1, local copies, waits for them, and re-layouts: 4.14 us -> 0.71 us
where the time goes in v2:
time: 55.3 us; the launch traced here: 55.2 us
  Pallas kernels  54.5 us (99%)
  local copies, waits for them, and re-layouts  0.71 us (1%)
    pallas_call x1, Pallas kernels, on_device(): pl.pallas_call(kernel, out_shape=pltpu.VMEM((16, 16, CYCLES), f32), in_sp...  54.5 us

profile of v2, /device:TPU:1, one launch (start us, length us, event | category | flops | bytes accessed | tf_op | source)
XLA Modules:
  0.0 55.2 jit_solution(4791313729610634286)
XLA Ops:
  0.0 54.5 %kam.1 = f32[16,16,256]{2,1,0:T(8,128)S(1)} custom-call(bf16[16,256,1024]{2,1,0:T(8,128)(2,1)} %img_hbm.1, s32[128,256]{1,0:T(8,128)} %msk_hbm.1, f32[1,128]{1,0:T(1,128)} %bitcast.1, f32[128,128]{1,0:T(8,128)} %inv_hbm.1, bf16[256,1024]{1,0:T(8,128)(2,1)} %constant.2.clone.tab_hbm), custom_call_target="tpu_custom_call" | custom-call | tf_op jit(solution)/shard_map/kam/pallas_call | solution.py:257
  54.5 0.7 %copy.7 = f32[16,16,256]{2,1,0:T(8,128)} copy(f32[16,16,256]{2,1,0:T(8,128)S(1)} %kam.1) | data formatting | bytes 524288

commit v3 on v2

v3 whole, which is shorter than its diff:
```python
import functools
import math

import jax
import jax.numpy as jnp
import numpy as np
from jax import lax
from jax.experimental import pallas as pl
from jax.experimental.pallas import tpu as pltpu
from jax.sharding import PartitionSpec as P

MESH = pl.DeviceIdType.MESH
SIDE = 4
GROUPS = SIDE * SIDE
LINE = 2 * SIDE
SNAPS = 16
CYCLES = 256
ANGLES = 1024
ORDERS = 128
HALF = ORDERS // 2
CHUNK = 4


def make_table():
    order_index = np.arange(ORDERS)
    angle_index = np.arange(ANGLES)
    phase_index = order_index[:, None] * angle_index[None, :] % ANGLES
    radians = phase_index.astype(np.float32) * np.float32(2.0 * math.pi / ANGLES)
    norming = np.float32(math.sqrt(2.0 / ANGLES))
    table = np.concatenate([np.cos(radians) * norming, -np.sin(radians) * norming], axis=0)
    return table.astype(jnp.bfloat16)


HOPS = sorted(
    [(hx, hy, hz) for hx in (2, 1, 0) for hy in (2, 1, 0) for hz in (2, 1, 0)], key=lambda hops: -sum(hops)
)


def for_each_offset(visit, cores=2, lines=True):
    for hops in HOPS:
        if not lines and hops[0]:
            continue
        first = 1 if sum(hops) == 0 else 0
        last = cores * 2 ** sum(h == 1 for h in hops)

        def step(k, carry, hops=hops):
            dc = k % cores
            signs = k // cores
            offsets = []
            for h in hops:
                if h == 1:
                    offsets.append(1 + 2 * (signs % 2))
                    signs = signs // 2
                else:
                    offsets.append(h)
            visit(offsets[0], dc, offsets[1], offsets[2])
            return carry

        if first < last:
            lax.fori_loop(first, last, step, 0)


SLOTS = sorted(
    [(dy, dz) for dy in range(SIDE) for dz in range(SIDE)],
    key=lambda offset: -sum(min(d, SIDE - d) for d in offset),
)


def kernel(
    img_hbm, msk_hbm, wts_hbm, inv_hbm, tab_hbm, out_ref,
    img, tab, msk, wts, inv, spectra, coeffs, arrived, counts, all_counts, all_wts, gram, tiles, kams,
    in_sems, img_sems, w_send, w_recv, a_send, a_recv, n_send, n_recv, g_send, g_recv, h_send, h_recv, k_send, k_recv,
):
    s = lax.axis_index("snap")
    o = lax.axis_index("ord")
    y, z = s // SIDE, s % SIDE
    x, c = o // 2, o % 2
    x_row, x_lane = x // 2, x % 2

    small = [
        pltpu.make_async_copy(src, dst, in_sems.at[k])
        for k, (src, dst) in enumerate(
            [(tab_hbm, tab), (msk_hbm, msk), (wts_hbm, wts), (inv_hbm, inv)]
        )
    ]
    small[0].start()
    for k in range(SNAPS // CHUNK):
        part = pl.ds(k * CHUNK, CHUNK)
        pltpu.make_async_copy(img_hbm.at[part], img.at[part], img_sems.at[k]).start()
        if k == 0:
            for copy in small[1:]:
                copy.start()

    barrier = pltpu.get_barrier_semaphore()

    def there(dx, dc, dy, dz):
        return ((y + dy) % SIDE) * SIDE + (z + dz) % SIDE, ((x + dx) % SIDE) * 2 + (c + dc) % 2

    def greet(*offset):
        pl.semaphore_signal(barrier, inc=1, device_id=there(*offset), device_id_type=MESH)

    for_each_offset(greet)

    for copy in small[1:]:
        copy.wait()
    mask = msk[...].astype(jnp.float32)
    mask_half = msk[:, pl.ds(pl.multiple_of(x_lane * 128, 128), 128)].astype(jnp.float32)
    counts[...] = jnp.dot(
        mask.T * wts[...], mask_half,
        precision=lax.Precision.HIGHEST, preferred_element_type=jnp.float32,
    )

    def count_tile(group):
        return counts.at[pl.ds(pl.multiple_of(16 * group + 8 * x_row, 8), 8), :]

    small[0].wait()

    def transform(chunk, carry):
        first = chunk * CHUNK
        loads = img.at[pl.ds(first, CHUNK)]
        pltpu.make_async_copy(loads, loads, img_sems.at[chunk]).wait()
        for u in range(CHUNK):
            k = first + u
            product = lax.dot_general(
                tab[...], img[k], (((1,), (1,)), ((), ())), preferred_element_type=jnp.float32
            )
            product = product * msk[pl.ds(o * SNAPS + k, 1), :].astype(jnp.float32)
            place = pl.multiple_of(k * 2 * ORDERS, 2 * ORDERS)
            for lane in range(2):
                spectra[lane, pl.ds(place, 2 * ORDERS), :] = product[:, 128 * lane : 128 * lane + 128]
        return carry

    lax.fori_loop(0, SNAPS // CHUNK, transform, 0)

    pl.semaphore_wait(barrier, GROUPS * LINE - 1)

    def send_weights(dx, dc, dy, dz):
        group, _ = there(0, 0, dy, dz)
        pltpu.make_async_remote_copy(
            wts, all_wts.at[SIDE * dy + dz], w_send, w_recv, device_id=(group, o), device_id_type=MESH
        ).start()

    for_each_offset(send_weights, cores=1, lines=False)
    all_wts[0] = wts[...]

    def gather(order):
        for part in range(2):
            for lane in range(2):
                rows = spectra[lane, pl.ds(part * ORDERS + order, SNAPS, stride=2 * ORDERS), :]
                coeffs[order, part, :, 128 * lane : 128 * lane + 128] = rows.astype(jnp.bfloat16)

    own_order = c * HALF + x * GROUPS + s
    gather(own_order)
    pltpu.make_async_copy(coeffs.at[own_order], arrived.at[0, :, o], a_recv.at[0]).start()

    def send_coeffs(*offset):
        group, line = there(*offset)
        order = (line % 2) * HALF + (line // 2) * GROUPS + group
        gather(order)
        slot = SIDE * offset[2] + offset[3]
        pltpu.make_async_remote_copy(
            coeffs.at[order], arrived.at[slot, :, o], a_send, a_recv.at[slot],
            device_id=(group, line), device_id_type=MESH,
        ).start()

    for_each_offset(send_coeffs)

    pltpu.make_async_copy(all_wts.at[pl.ds(1, 15)], all_wts.at[pl.ds(1, 15)], w_recv).wait()
    gram[...] = jnp.zeros_like(gram)

    for dy, dz in SLOTS:
        slot = SIDE * dy + dz
        pltpu.make_async_copy(arrived.at[slot], arrived.at[slot], a_recv.at[slot]).wait()
        block = arrived[slot].reshape(2 * LINE * SNAPS, CYCLES)
        weight = jnp.concatenate([all_wts[slot], all_wts[slot]], axis=1)
        weighted = (block.astype(jnp.float32).T * weight).astype(jnp.bfloat16)
        gram[...] += jnp.dot(weighted, block, preferred_element_type=jnp.float32)

    tile_rows = pl.ds(pl.multiple_of(8 * own_order, 8), 8)

    def gram_tile(group, chip):
        row = pl.multiple_of(16 * group + 8 * (chip // 2), 8)
        lane = pl.multiple_of(128 * (chip % 2), 128)
        return gram.at[pl.ds(row, 8), pl.ds(lane, 128)]

    pltpu.make_async_copy(gram_tile(s, x), tiles.at[tile_rows], g_recv.at[0]).start()

    def send_tile(dx, dc, dy, dz):
        group, line = there(dx, 0, dy, dz)
        pltpu.make_async_remote_copy(
            gram_tile(group, line // 2), tiles.at[tile_rows], g_send, g_recv.at[dx],
            device_id=(group, line), device_id_type=MESH,
        ).start()

    for_each_offset(send_tile, cores=1)

    def send_count(dx, dc, dy, dz):
        group, _ = there(0, 0, dy, dz)
        pltpu.make_async_remote_copy(
            count_tile(group), all_counts.at[SIDE * dy + dz], n_send, n_recv,
            device_id=(group, o), device_id_type=MESH,
        ).start()

    for_each_offset(send_count, cores=1, lines=False)
    pltpu.make_async_copy(count_tile(s), all_counts.at[0], n_recv).start()

    for wave in range(SIDE):
        dx = (2, 1, 3, 0)[wave]
        row = pl.multiple_of(8 * (c * HALF + ((x + SIDE - dx) % SIDE) * GROUPS), 8 * GROUPS)
        part = tiles.at[pl.ds(row, 8 * GROUPS)]
        pltpu.make_async_copy(part, part, g_recv.at[dx]).wait()
        swap = pltpu.make_async_remote_copy(
            part, part, h_send, h_recv, device_id=(s, x * 2 + 1 - c), device_id_type=MESH
        )
        swap.start()
    own_inv = jnp.concatenate(
        [inv[pl.ds(pl.multiple_of(32 * k + 16 * c, 16), 16), :] for k in range(SIDE)], axis=0
    )
    own_half = tiles.at[pl.ds(pl.multiple_of(8 * HALF * c, 8 * HALF), 8 * HALF)]
    other_half = tiles.at[pl.ds(pl.multiple_of(8 * HALF * (1 - c), 8 * HALF), 8 * HALF)]
    pltpu.make_async_copy(own_half, own_half, h_send).wait()
    pltpu.make_async_copy(other_half, other_half, h_recv).wait()

    pltpu.make_async_copy(all_counts, all_counts, n_recv).wait()
    count = jnp.maximum(jnp.sum(all_counts[...], axis=0), 1.0)

    flat_kams = kams.reshape(HALF * 8, 128)
    for r in range(8):
        grams = tiles[pl.ds(r, ORDERS, stride=8), :]
        correl = grams / count[r : r + 1, :]
        flat_kams[pl.ds(r, HALF, stride=8), :] = jnp.dot(
            own_inv, correl, precision=lax.Precision.HIGHEST, preferred_element_type=jnp.float32
        )

    place = out_ref.at[:, pl.ds(pl.multiple_of(8 * x_row, 8), 8), pl.ds(pl.multiple_of(128 * x_lane, 128), 128)]
    for d in (2, 1, 3):
        there_x = (x + d) % SIDE
        pltpu.make_async_remote_copy(
            kams.at[pl.ds(16 * there_x, 16)], place, k_send, k_recv,
            device_id=(s, there_x * 2 + c), device_id_type=MESH,
        ).start()
    pltpu.make_async_copy(kams.at[pl.ds(16 * x, 16)], place, k_recv).start()

    pltpu.make_async_copy(all_wts.at[pl.ds(0, 15)], all_wts.at[pl.ds(0, 15)], w_send).wait()
    pltpu.make_async_copy(all_counts.at[pl.ds(0, 15)], all_counts.at[pl.ds(0, 15)], n_send).wait()
    pltpu.make_async_copy(coeffs.at[pl.ds(0, 127)], coeffs.at[pl.ds(0, 127)], a_send).wait()
    pltpu.make_async_copy(tiles.at[pl.ds(0, 504)], tiles.at[pl.ds(0, 504)], g_send).wait()
    pltpu.make_async_copy(kams.at[pl.ds(0, 48)], kams.at[pl.ds(0, 48)], k_send).wait()
    pltpu.make_async_copy(out_ref, out_ref, k_recv).wait()


def on_device(images, cycle_masks, weights, inversion):
    operands = (images, cycle_masks, weights.reshape(1, -1), inversion, jnp.asarray(make_table()))
    dma = pltpu.SemaphoreType.DMA
    f32, bf16 = jnp.float32, jnp.bfloat16
    return pl.pallas_call(
        kernel,
        out_shape=pltpu.VMEM((16, 16, CYCLES), f32),
        in_specs=[pl.BlockSpec(memory_space=pltpu.HBM)] * 5,
        out_specs=pl.BlockSpec(memory_space=pltpu.VMEM),
        scratch_shapes=[
            pltpu.VMEM((SNAPS, CYCLES, ANGLES), bf16),
            pltpu.VMEM((2 * ORDERS, ANGLES), bf16),
            pltpu.VMEM((LINE * SNAPS, CYCLES), jnp.int32),
            pltpu.VMEM((1, LINE * SNAPS), f32),
            pltpu.VMEM((ORDERS, ORDERS), f32),
            pltpu.VMEM((2, SNAPS * 2 * ORDERS, 128), f32),
            pltpu.VMEM((ORDERS, 2, SNAPS, CYCLES), bf16),
            pltpu.VMEM((GROUPS, 2, LINE, SNAPS, CYCLES), bf16),
            pltpu.VMEM((CYCLES, 128), f32),
            pltpu.VMEM((GROUPS, 8, 128), f32),
            pltpu.VMEM((GROUPS, 1, LINE * SNAPS), f32),
            pltpu.VMEM((CYCLES, CYCLES), f32),
            pltpu.VMEM((ORDERS * 8, 128), f32),
            pltpu.VMEM((HALF, 8, 128), f32),
            dma((4,)),
            dma((SNAPS // CHUNK,)),
            dma, dma, dma,
            dma((GROUPS,)),
            dma, dma, dma,
            dma((SIDE,)),
            dma, dma, dma, dma,
        ],
        compiler_params=pltpu.CompilerParams(
            collective_id=0, has_side_effects=True, vmem_limit_bytes=48 * 2**20
        ),
        name="kam",
    )(*(pltpu.with_memory_space_constraint(value, pltpu.HBM) for value in operands))


def solution(mesh):
    placed = (P(("snap", "ord"), None, None), P("snap", None), P("snap"), P())
    return jax.shard_map(
        on_device, mesh=mesh, in_specs=placed, out_specs=P("ord", "snap", None), check_vma=False
    )
```

time: 55.3 us -> 57.4 us (1.038)
  Pallas kernels: 54.5 us -> 56.6 us
    pallas_call x1, Pallas kernels: 54.5 us -> 56.6 us  [on_device(): pl.pallas_call(kernel, out_shape=pltpu.VMEM((16, 16, CYCLES), f32), in_sp...]
where the time goes in v3:
time: 57.4 us; the launch traced here: 57.3 us
  Pallas kernels  56.6 us (99%)
  local copies, waits for them, and re-layouts  0.71 us (1%)
    pallas_call x1, Pallas kernels, on_device(): pl.pallas_call(kernel, out_shape=pltpu.VMEM((16, 16, CYCLES), f32), in_sp...  56.6 us

profile of v3, /device:TPU:1, one launch (start us, length us, event | category | flops | bytes accessed | tf_op | source)
XLA Modules:
  0.0 57.3 jit_solution(1362432516595874840)
XLA Ops:
  0.0 56.6 %kam.1 = f32[16,16,256]{2,1,0:T(8,128)S(1)} custom-call(bf16[16,256,1024]{2,1,0:T(8,128)(2,1)} %img_hbm.1, s32[128,256]{1,0:T(8,128)} %msk_hbm.1, f32[1,128]{1,0:T(1,128)} %bitcast.1, f32[128,128]{1,0:T(8,128)} %inv_hbm.1, bf16[256,1024]{1,0:T(8,128)(2,1)} %constant.2.clone.tab_hbm), custom_call_target="tpu_custom_call" | custom-call | tf_op jit(solution)/shard_map/kam/pallas_call | solution.py:256
  56.6 0.7 %copy.7 = f32[16,16,256]{2,1,0:T(8,128)} copy(f32[16,16,256]{2,1,0:T(8,128)S(1)} %kam.1) | data formatting | bytes 524288

commit v4 on v3

--- a/solution.py
+++ b/solution.py
@@ -32,20 +32,16 @@
 
 
 HOPS = sorted(
-    [(hx, hy, hz) for hx in (2, 1, 0) for hy in (2, 1, 0) for hz in (2, 1, 0)], key=lambda hops: -sum(hops)
+    [(hx, hy, hz) for hx in (2, 1, 0) for hy in (2, 1, 0) for hz in (2, 1, 0)],
+    key=lambda hops: (-hops[1] - hops[2], -hops[0]),
 )
 
 
-def for_each_offset(visit, cores=2, lines=True):
+def for_each_offset(visit):
     for hops in HOPS:
-        if not lines and hops[0]:
-            continue
-        first = 1 if sum(hops) == 0 else 0
-        last = cores * 2 ** sum(h == 1 for h in hops)
 
         def step(k, carry, hops=hops):
-            dc = k % cores
-            signs = k // cores
+            signs = k // 2
             offsets = []
             for h in hops:
                 if h == 1:
@@ -53,16 +49,20 @@
                     signs = signs // 2
                 else:
                     offsets.append(h)
-            visit(offsets[0], dc, offsets[1], offsets[2])
+            visit(offsets[0], k % 2, offsets[1], offsets[2])
             return carry
 
-        if first < last:
-            lax.fori_loop(first, last, step, 0)
-
+        lax.fori_loop(0 if sum(hops) else 1, 2 * 2 ** sum(h == 1 for h in hops), step, 0)
+
+
+CHIPS = sorted(
+    [(dx, dy, dz) for dx in range(SIDE) for dy in range(SIDE) for dz in range(SIDE) if dx + dy + dz],
+    key=lambda offset: -sum(min(d, SIDE - d) for d in offset),
+)
 
 SLOTS = sorted(
     [(dy, dz) for dy in range(SIDE) for dz in range(SIDE)],
-    key=lambda offset: -sum(min(d, SIDE - d) for d in offset),
+    key=lambda offset: [-sum(min(d, SIDE - d) for d in offset)] + [-min(d, SIDE - d) for d in offset],
 )
 
 
@@ -91,29 +91,18 @@
             for copy in small[1:]:
                 copy.start()
 
+    x_at = [(x + d) % SIDE for d in range(SIDE)]
+    y_at = [(y + d) % SIDE * SIDE for d in range(SIDE)]
+    z_at = [(z + d) % SIDE for d in range(SIDE)]
     barrier = pltpu.get_barrier_semaphore()
-
-    def there(dx, dc, dy, dz):
-        return ((y + dy) % SIDE) * SIDE + (z + dz) % SIDE, ((x + dx) % SIDE) * 2 + (c + dc) % 2
-
-    def greet(*offset):
-        pl.semaphore_signal(barrier, inc=1, device_id=there(*offset), device_id_type=MESH)
-
-    for_each_offset(greet)
-
-    for copy in small[1:]:
+    for dx, dy, dz in CHIPS + [(0, 0, 0)]:
+        for dc in (0, 1):
+            if dx or dy or dz or dc:
+                there = (y_at[dy] + z_at[dz], x_at[dx] * 2 + (c if dc == 0 else 1 - c))
+                pl.semaphore_signal(barrier, inc=1, device_id=there, device_id_type=MESH)
+
+    for copy in small[:3]:
         copy.wait()
-    mask = msk[...].astype(jnp.float32)
-    mask_half = msk[:, pl.ds(pl.multiple_of(x_lane * 128, 128), 128)].astype(jnp.float32)
-    counts[...] = jnp.dot(
-        mask.T * wts[...], mask_half,
-        precision=lax.Precision.HIGHEST, preferred_element_type=jnp.float32,
-    )
-
-    def count_tile(group):
-        return counts.at[pl.ds(pl.multiple_of(16 * group + 8 * x_row, 8), 8), :]
-
-    small[0].wait()
 
     def transform(chunk, carry):
         first = chunk * CHUNK
@@ -134,13 +123,12 @@
 
     pl.semaphore_wait(barrier, GROUPS * LINE - 1)
 
-    def send_weights(dx, dc, dy, dz):
-        group, _ = there(0, 0, dy, dz)
-        pltpu.make_async_remote_copy(
-            wts, all_wts.at[SIDE * dy + dz], w_send, w_recv, device_id=(group, o), device_id_type=MESH
-        ).start()
-
-    for_each_offset(send_weights, cores=1, lines=False)
+    for dx, dy, dz in CHIPS:
+        if dx == 0:
+            pltpu.make_async_remote_copy(
+                wts, all_wts.at[SIDE * dy + dz], w_send, w_recv,
+                device_id=(y_at[dy] + z_at[dz], o), device_id_type=MESH,
+            ).start()
     all_wts[0] = wts[...]
 
     def gather(order):
@@ -153,17 +141,29 @@
     gather(own_order)
     pltpu.make_async_copy(coeffs.at[own_order], arrived.at[0, :, o], a_recv.at[0]).start()
 
-    def send_coeffs(*offset):
-        group, line = there(*offset)
-        order = (line % 2) * HALF + (line // 2) * GROUPS + group
+    def send_coeffs(dx, dc, dy, dz):
+        group = (y + dy) % SIDE * SIDE + (z + dz) % SIDE
+        there_x, there_c = (x + dx) % SIDE, (c + dc) % 2
+        order = there_c * HALF + there_x * GROUPS + group
         gather(order)
-        slot = SIDE * offset[2] + offset[3]
+        slot = SIDE * dy + dz
         pltpu.make_async_remote_copy(
             coeffs.at[order], arrived.at[slot, :, o], a_send, a_recv.at[slot],
-            device_id=(group, line), device_id_type=MESH,
+            device_id=(group, there_x * 2 + there_c), device_id_type=MESH,
         ).start()
 
     for_each_offset(send_coeffs)
+
+    small[3].wait()
+    mask = msk[...].astype(jnp.float32)
+    mask_half = msk[:, pl.ds(pl.multiple_of(x_lane * 128, 128), 128)].astype(jnp.float32)
+    counts[...] = jnp.dot(
+        mask.T * wts[...], mask_half,
+        precision=lax.Precision.HIGHEST, preferred_element_type=jnp.float32,
+    )
+
+    def count_tile(group):
+        return counts.at[pl.ds(pl.multiple_of(16 * group + 8 * x_row, 8), 8), :]
 
     pltpu.make_async_copy(all_wts.at[pl.ds(1, 15)], all_wts.at[pl.ds(1, 15)], w_recv).wait()
     gram[...] = jnp.zeros_like(gram)
@@ -183,25 +183,22 @@
         lane = pl.multiple_of(128 * (chip % 2), 128)
         return gram.at[pl.ds(row, 8), pl.ds(lane, 128)]
 
+    for dx, dy, dz in CHIPS:
+        there_x = x_at[dx]
+        group = y_at[dy] + z_at[dz]
+        pltpu.make_async_remote_copy(
+            gram_tile(group, there_x), tiles.at[tile_rows], g_send, g_recv.at[dx],
+            device_id=(group, there_x * 2 + c), device_id_type=MESH,
+        ).start()
     pltpu.make_async_copy(gram_tile(s, x), tiles.at[tile_rows], g_recv.at[0]).start()
 
-    def send_tile(dx, dc, dy, dz):
-        group, line = there(dx, 0, dy, dz)
-        pltpu.make_async_remote_copy(
-            gram_tile(group, line // 2), tiles.at[tile_rows], g_send, g_recv.at[dx],
-            device_id=(group, line), device_id_type=MESH,
-        ).start()
-
-    for_each_offset(send_tile, cores=1)
-
-    def send_count(dx, dc, dy, dz):
-        group, _ = there(0, 0, dy, dz)
-        pltpu.make_async_remote_copy(
-            count_tile(group), all_counts.at[SIDE * dy + dz], n_send, n_recv,
-            device_id=(group, o), device_id_type=MESH,
-        ).start()
-
-    for_each_offset(send_count, cores=1, lines=False)
+    for dx, dy, dz in CHIPS:
+        if dx == 0:
+            group = y_at[dy] + z_at[dz]
+            pltpu.make_async_remote_copy(
+                count_tile(group), all_counts.at[SIDE * dy + dz], n_send, n_recv,
+                device_id=(group, o), device_id_type=MESH,
+            ).start()
     pltpu.make_async_copy(count_tile(s), all_counts.at[0], n_recv).start()
 
     for wave in range(SIDE):

time: 57.4 us -> 54 us (0.941)
  Pallas kernels: 56.6 us -> 53.2 us
    pallas_call x1, Pallas kernels: 56.6 us -> 53.2 us  [on_device(): pl.pallas_call(kernel, out_shape=pltpu.VMEM((16, 16, CYCLES), f32), in_sp...]
where the time goes in v4:
time: 54 us; the launch traced here: 53.9 us
  Pallas kernels  53.2 us (99%)
  local copies, waits for them, and re-layouts  0.71 us (1%)
    pallas_call x1, Pallas kernels, on_device(): pl.pallas_call(kernel, out_shape=pltpu.VMEM((16, 16, CYCLES), f32), in_sp...  53.2 us

profile of v4, /device:TPU:1, one launch (start us, length us, event | category | flops | bytes accessed | tf_op | source)
XLA Modules:
  0.0 53.9 jit_solution(5687883424054269407)
XLA Ops:
  0.0 53.2 %kam.1 = f32[16,16,256]{2,1,0:T(8,128)S(1)} custom-call(bf16[16,256,1024]{2,1,0:T(8,128)(2,1)} %img_hbm.1, s32[128,256]{1,0:T(8,128)} %msk_hbm.1, f32[1,128]{1,0:T(1,128)} %bitcast.1, f32[128,128]{1,0:T(8,128)} %inv_hbm.1, bf16[256,1024]{1,0:T(8,128)(2,1)} %constant.2.clone.tab_hbm), custom_call_target="tpu_custom_call" | custom-call | tf_op jit(solution)/shard_map/kam/pallas_call | solution.py:253
  53.2 0.7 %copy.7 = f32[16,16,256]{2,1,0:T(8,128)} copy(f32[16,16,256]{2,1,0:T(8,128)S(1)} %kam.1) | data formatting | bytes 524288

commit v5 on v4

--- a/solution.py
+++ b/solution.py
@@ -49,7 +49,9 @@
                     signs = signs // 2
                 else:
                     offsets.append(h)
-            visit(offsets[0], k % 2, offsets[1], offsets[2])
+            sign_y, sign_z = [d // 3 if h == 1 else 0 for d, h in zip(offsets[1:], hops[1:])]
+            slot = SLOT_BASE[hops[1:]] + sign_y + (2 if hops[1] == 1 else 1) * sign_z
+            visit(offsets[0], k % 2, offsets[1], offsets[2], slot)
             return carry
 
         lax.fori_loop(0 if sum(hops) else 1, 2 * 2 ** sum(h == 1 for h in hops), step, 0)
@@ -60,10 +62,20 @@
     key=lambda offset: -sum(min(d, SIDE - d) for d in offset),
 )
 
-SLOTS = sorted(
-    [(dy, dz) for dy in range(SIDE) for dz in range(SIDE)],
-    key=lambda offset: [-sum(min(d, SIDE - d) for d in offset)] + [-min(d, SIDE - d) for d in offset],
-)
+SLOT_BASE = {}
+for _, hop_y, hop_z in HOPS:
+    if (hop_y, hop_z) not in SLOT_BASE:
+        SLOT_BASE[hop_y, hop_z] = sum(2 ** ((u == 1) + (v == 1)) for u, v in SLOT_BASE)
+RUNS = ((0, 1), (1, 4), (5, 6), (11, 5))
+
+
+OWN_SLOT = GROUPS - 1
+
+
+def slot_of(dy, dz):
+    hop_y, hop_z = min(dy, SIDE - dy), min(dz, SIDE - dz)
+    sign_y, sign_z = dy // 3, dz // 3
+    return SLOT_BASE[hop_y, hop_z] + sign_y + (2 if hop_y == 1 else 1) * sign_z
 
 
 def kernel(
@@ -126,10 +138,10 @@
     for dx, dy, dz in CHIPS:
         if dx == 0:
             pltpu.make_async_remote_copy(
-                wts, all_wts.at[SIDE * dy + dz], w_send, w_recv,
+                wts, all_wts.at[slot_of(dy, dz)], w_send, w_recv,
                 device_id=(y_at[dy] + z_at[dz], o), device_id_type=MESH,
             ).start()
-    all_wts[0] = wts[...]
+    all_wts[OWN_SLOT] = wts[...]
 
     def gather(order):
         for part in range(2):
@@ -139,14 +151,13 @@
 
     own_order = c * HALF + x * GROUPS + s
     gather(own_order)
-    pltpu.make_async_copy(coeffs.at[own_order], arrived.at[0, :, o], a_recv.at[0]).start()
-
-    def send_coeffs(dx, dc, dy, dz):
+    pltpu.make_async_copy(coeffs.at[own_order], arrived.at[OWN_SLOT, :, o], a_recv.at[OWN_SLOT]).start()
+
+    def send_coeffs(dx, dc, dy, dz, slot):
         group = (y + dy) % SIDE * SIDE + (z + dz) % SIDE
         there_x, there_c = (x + dx) % SIDE, (c + dc) % 2
         order = there_c * HALF + there_x * GROUPS + group
         gather(order)
-        slot = SIDE * dy + dz
         pltpu.make_async_remote_copy(
             coeffs.at[order], arrived.at[slot, :, o], a_send, a_recv.at[slot],
             device_id=(group, there_x * 2 + there_c), device_id_type=MESH,
@@ -165,16 +176,16 @@
     def count_tile(group):
         return counts.at[pl.ds(pl.multiple_of(16 * group + 8 * x_row, 8), 8), :]
 
-    pltpu.make_async_copy(all_wts.at[pl.ds(1, 15)], all_wts.at[pl.ds(1, 15)], w_recv).wait()
-    gram[...] = jnp.zeros_like(gram)
-
-    for dy, dz in SLOTS:
-        slot = SIDE * dy + dz
-        pltpu.make_async_copy(arrived.at[slot], arrived.at[slot], a_recv.at[slot]).wait()
-        block = arrived[slot].reshape(2 * LINE * SNAPS, CYCLES)
-        weight = jnp.concatenate([all_wts[slot], all_wts[slot]], axis=1)
-        weighted = (block.astype(jnp.float32).T * weight).astype(jnp.bfloat16)
-        gram[...] += jnp.dot(weighted, block, preferred_element_type=jnp.float32)
+    pltpu.make_async_copy(all_wts.at[pl.ds(0, 15)], all_wts.at[pl.ds(0, 15)], w_recv).wait()
+
+    for first, count in RUNS:
+        for slot in range(first, first + count):
+            pltpu.make_async_copy(arrived.at[slot], arrived.at[slot], a_recv.at[slot]).wait()
+        block = arrived[first : first + count].reshape(count * 2 * LINE * SNAPS, CYCLES)
+        weight = jnp.concatenate([all_wts[first + k // 2] for k in range(2 * count)], axis=1)
+        weighted = (block.T.astype(jnp.float32) * weight).astype(jnp.bfloat16)
+        product = jnp.dot(weighted, block, preferred_element_type=jnp.float32)
+        gram[...] = product if first == 0 else gram[...] + product
 
     tile_rows = pl.ds(pl.multiple_of(8 * own_order, 8), 8)
 
@@ -196,10 +207,10 @@
         if dx == 0:
             group = y_at[dy] + z_at[dz]
             pltpu.make_async_remote_copy(
-                count_tile(group), all_counts.at[SIDE * dy + dz], n_send, n_recv,
+                count_tile(group), all_counts.at[slot_of(dy, dz)], n_send, n_recv,
                 device_id=(group, o), device_id_type=MESH,
             ).start()
-    pltpu.make_async_copy(count_tile(s), all_counts.at[0], n_recv).start()
+    pltpu.make_async_copy(count_tile(s), all_counts.at[OWN_SLOT], n_recv).start()
 
     for wave in range(SIDE):
         dx = (2, 1, 3, 0)[wave]

time: 54 us -> 53.4 us (0.989)
  Pallas kernels: 53.2 us -> 52.6 us
    pallas_call x1, Pallas kernels: 53.2 us -> 52.6 us  [on_device(): pl.pallas_call(kernel, out_shape=pltpu.VMEM((16, 16, CYCLES), f32), in_sp...]
where the time goes in v5:
time: 53.4 us; the launch traced here: 53.3 us
  Pallas kernels  52.6 us (99%)
  local copies, waits for them, and re-layouts  0.71 us (1%)
    pallas_call x1, Pallas kernels, on_device(): pl.pallas_call(kernel, out_shape=pltpu.VMEM((16, 16, CYCLES), f32), in_sp...  52.6 us

profile of v5, /device:TPU:1, one launch (start us, length us, event | category | flops | bytes accessed | tf_op | source)
XLA Modules:
  0.0 53.3 jit_solution(4928283304401899203)
XLA Ops:
  0.0 52.6 %kam.1 = f32[16,16,256]{2,1,0:T(8,128)S(1)} custom-call(bf16[16,256,1024]{2,1,0:T(8,128)(2,1)} %img_hbm.1, s32[128,256]{1,0:T(8,128)} %msk_hbm.1, f32[1,128]{1,0:T(1,128)} %bitcast.1, f32[128,128]{1,0:T(8,128)} %inv_hbm.1, bf16[256,1024]{1,0:T(8,128)(2,1)} %constant.2.clone.tab_hbm), custom_call_target="tpu_custom_call" | custom-call | tf_op jit(solution)/shard_map/kam/pallas_call | solution.py:264
  52.6 0.7 %copy.7 = f32[16,16,256]{2,1,0:T(8,128)} copy(f32[16,16,256]{2,1,0:T(8,128)S(1)} %kam.1) | data formatting | bytes 524288

commit v6 on v5

--- a/solution.py
+++ b/solution.py
@@ -226,19 +226,18 @@
     )
     own_half = tiles.at[pl.ds(pl.multiple_of(8 * HALF * c, 8 * HALF), 8 * HALF)]
     other_half = tiles.at[pl.ds(pl.multiple_of(8 * HALF * (1 - c), 8 * HALF), 8 * HALF)]
-    pltpu.make_async_copy(own_half, own_half, h_send).wait()
     pltpu.make_async_copy(other_half, other_half, h_recv).wait()
 
     pltpu.make_async_copy(all_counts, all_counts, n_recv).wait()
     count = jnp.maximum(jnp.sum(all_counts[...], axis=0), 1.0)
 
+    correl = jnp.concatenate(
+        [tiles[pl.ds(r, ORDERS, stride=8), :] / count[r : r + 1, :] for r in range(8)], axis=1
+    )
+    product = jnp.dot(own_inv, correl, precision=lax.Precision.HIGHEST, preferred_element_type=jnp.float32)
     flat_kams = kams.reshape(HALF * 8, 128)
     for r in range(8):
-        grams = tiles[pl.ds(r, ORDERS, stride=8), :]
-        correl = grams / count[r : r + 1, :]
-        flat_kams[pl.ds(r, HALF, stride=8), :] = jnp.dot(
-            own_inv, correl, precision=lax.Precision.HIGHEST, preferred_element_type=jnp.float32
-        )
+        flat_kams[pl.ds(r, HALF, stride=8), :] = product[:, 128 * r : 128 * r + 128]
 
     place = out_ref.at[:, pl.ds(pl.multiple_of(8 * x_row, 8), 8), pl.ds(pl.multiple_of(128 * x_lane, 128), 128)]
     for d in (2, 1, 3):
@@ -253,6 +252,7 @@
     pltpu.make_async_copy(all_counts.at[pl.ds(0, 15)], all_counts.at[pl.ds(0, 15)], n_send).wait()
     pltpu.make_async_copy(coeffs.at[pl.ds(0, 127)], coeffs.at[pl.ds(0, 127)], a_send).wait()
     pltpu.make_async_copy(tiles.at[pl.ds(0, 504)], tiles.at[pl.ds(0, 504)], g_send).wait()
+    pltpu.make_async_copy(own_half, own_half, h_send).wait()
     pltpu.make_async_copy(kams.at[pl.ds(0, 48)], kams.at[pl.ds(0, 48)], k_send).wait()
     pltpu.make_async_copy(out_ref, out_ref, k_recv).wait()
 

time: 53.4 us -> 52.6 us (0.985)
  Pallas kernels: 52.6 us -> 51.8 us
    pallas_call x1, Pallas kernels: 52.6 us -> 51.8 us  [on_device(): pl.pallas_call(kernel, out_shape=pltpu.VMEM((16, 16, CYCLES), f32), in_sp...]
where the time goes in v6:
time: 52.6 us; the launch traced here: 52.5 us
  Pallas kernels  51.8 us (98%)
  local copies, waits for them, and re-layouts  0.71 us (1%)
    pallas_call x1, Pallas kernels, on_device(): pl.pallas_call(kernel, out_shape=pltpu.VMEM((16, 16, CYCLES), f32), in_sp...  51.8 us

profile of v6, /device:TPU:1, one launch (start us, length us, event | category | flops | bytes accessed | tf_op | source)
XLA Modules:
  0.0 52.5 jit_solution(11644314345059884408)
XLA Ops:
  0.0 51.8 %kam.1 = f32[16,16,256]{2,1,0:T(8,128)S(1)} custom-call(bf16[16,256,1024]{2,1,0:T(8,128)(2,1)} %img_hbm.1, s32[128,256]{1,0:T(8,128)} %msk_hbm.1, f32[1,128]{1,0:T(1,128)} %bitcast.1, f32[128,128]{1,0:T(8,128)} %inv_hbm.1, bf16[256,1024]{1,0:T(8,128)(2,1)} %constant.2.clone.tab_hbm), custom_call_target="tpu_custom_call" | custom-call | tf_op jit(solution)/shard_map/kam/pallas_call | solution.py:264
  51.8 0.7 %copy.7 = f32[16,16,256]{2,1,0:T(8,128)} copy(f32[16,16,256]{2,1,0:T(8,128)S(1)} %kam.1) | data formatting | bytes 524288

commit v7 on v6

--- a/solution.py
+++ b/solution.py
@@ -37,8 +37,11 @@
 )
 
 
-def for_each_offset(visit):
-    for hops in HOPS:
+FAR_HOPS, NEAR_HOPS = HOPS[:9], HOPS[9:]
+
+
+def for_each_offset(visit, order):
+    for hops in order:
 
         def step(k, carry, hops=hops):
             signs = k // 2
@@ -135,12 +138,6 @@
 
     pl.semaphore_wait(barrier, GROUPS * LINE - 1)
 
-    for dx, dy, dz in CHIPS:
-        if dx == 0:
-            pltpu.make_async_remote_copy(
-                wts, all_wts.at[slot_of(dy, dz)], w_send, w_recv,
-                device_id=(y_at[dy] + z_at[dz], o), device_id_type=MESH,
-            ).start()
     all_wts[OWN_SLOT] = wts[...]
 
     def gather(order):
@@ -150,8 +147,6 @@
                 coeffs[order, part, :, 128 * lane : 128 * lane + 128] = rows.astype(jnp.bfloat16)
 
     own_order = c * HALF + x * GROUPS + s
-    gather(own_order)
-    pltpu.make_async_copy(coeffs.at[own_order], arrived.at[OWN_SLOT, :, o], a_recv.at[OWN_SLOT]).start()
 
     def send_coeffs(dx, dc, dy, dz, slot):
         group = (y + dy) % SIDE * SIDE + (z + dz) % SIDE
@@ -163,7 +158,16 @@
             device_id=(group, there_x * 2 + there_c), device_id_type=MESH,
         ).start()
 
-    for_each_offset(send_coeffs)
+    for_each_offset(send_coeffs, FAR_HOPS)
+    for dx, dy, dz in CHIPS:
+        if dx == 0:
+            pltpu.make_async_remote_copy(
+                wts, all_wts.at[slot_of(dy, dz)], w_send, w_recv,
+                device_id=(y_at[dy] + z_at[dz], o), device_id_type=MESH,
+            ).start()
+    for_each_offset(send_coeffs, NEAR_HOPS)
+    gather(own_order)
+    pltpu.make_async_copy(coeffs.at[own_order], arrived.at[OWN_SLOT, :, o], a_recv.at[OWN_SLOT]).start()
 
     small[3].wait()
     mask = msk[...].astype(jnp.float32)
@@ -226,10 +230,10 @@
     )
     own_half = tiles.at[pl.ds(pl.multiple_of(8 * HALF * c, 8 * HALF), 8 * HALF)]
     other_half = tiles.at[pl.ds(pl.multiple_of(8 * HALF * (1 - c), 8 * HALF), 8 * HALF)]
-    pltpu.make_async_copy(other_half, other_half, h_recv).wait()
-
     pltpu.make_async_copy(all_counts, all_counts, n_recv).wait()
     count = jnp.maximum(jnp.sum(all_counts[...], axis=0), 1.0)
+    pltpu.make_async_copy(other_half, other_half, h_recv).wait()
+
 
     correl = jnp.concatenate(
         [tiles[pl.ds(r, ORDERS, stride=8), :] / count[r : r + 1, :] for r in range(8)], axis=1

time: 52.6 us -> 52.4 us (level)
  no operation moved by 1% of the time
where the time goes in v7:
time: 52.4 us; the launch traced here: 52.3 us
  Pallas kernels  51.5 us (98%)
  local copies, waits for them, and re-layouts  0.71 us (1%)
    pallas_call x1, Pallas kernels, on_device(): pl.pallas_call(kernel, out_shape=pltpu.VMEM((16, 16, CYCLES), f32), in_sp...  51.5 us

profile of v7, /device:TPU:1, one launch (start us, length us, event | category | flops | bytes accessed | tf_op | source)
XLA Modules:
  0.0 52.3 jit_solution(7602505373737686878)
XLA Ops:
  0.0 51.5 %kam.1 = f32[16,16,256]{2,1,0:T(8,128)S(1)} custom-call(bf16[16,256,1024]{2,1,0:T(8,128)(2,1)} %img_hbm.1, s32[128,256]{1,0:T(8,128)} %msk_hbm.1, f32[1,128]{1,0:T(1,128)} %bitcast.1, f32[128,128]{1,0:T(8,128)} %inv_hbm.1, bf16[256,1024]{1,0:T(8,128)(2,1)} %constant.2.clone.tab_hbm), custom_call_target="tpu_custom_call" | custom-call | tf_op jit(solution)/shard_map/kam/pallas_call | solution.py:268
  51.6 0.7 %copy.7 = f32[16,16,256]{2,1,0:T(8,128)} copy(f32[16,16,256]{2,1,0:T(8,128)S(1)} %kam.1) | data formatting | bytes 524288

commit v8 on v7

--- a/solution.py
+++ b/solution.py
@@ -98,6 +98,19 @@
             [(tab_hbm, tab), (msk_hbm, msk), (wts_hbm, wts), (inv_hbm, inv)]
         )
     ]
+    x_at = [(x + d) % SIDE for d in range(SIDE)]
+    y_at = [(y + d) % SIDE * SIDE for d in range(SIDE)]
+    z_at = [(z + d) % SIDE for d in range(SIDE)]
+    barrier = pltpu.get_barrier_semaphore()
+
+    def greet(chips):
+        for dx, dy, dz in chips:
+            for dc in (0, 1):
+                if dx or dy or dz or dc:
+                    there = (y_at[dy] + z_at[dz], x_at[dx] * 2 + (c if dc == 0 else 1 - c))
+                    pl.semaphore_signal(barrier, inc=1, device_id=there, device_id_type=MESH)
+
+    greet(CHIPS[:7])
     small[0].start()
     for k in range(SNAPS // CHUNK):
         part = pl.ds(k * CHUNK, CHUNK)
@@ -105,16 +118,7 @@
         if k == 0:
             for copy in small[1:]:
                 copy.start()
-
-    x_at = [(x + d) % SIDE for d in range(SIDE)]
-    y_at = [(y + d) % SIDE * SIDE for d in range(SIDE)]
-    z_at = [(z + d) % SIDE for d in range(SIDE)]
-    barrier = pltpu.get_barrier_semaphore()
-    for dx, dy, dz in CHIPS + [(0, 0, 0)]:
-        for dc in (0, 1):
-            if dx or dy or dz or dc:
-                there = (y_at[dy] + z_at[dz], x_at[dx] * 2 + (c if dc == 0 else 1 - c))
-                pl.semaphore_signal(barrier, inc=1, device_id=there, device_id_type=MESH)
+    greet(CHIPS[7:] + [(0, 0, 0)])
 
     for copy in small[:3]:
         copy.wait()

time: 52.4 us -> 53.1 us (1.013)
  Pallas kernels: 51.5 us -> 52.3 us
    pallas_call x1, Pallas kernels: 51.5 us -> 52.3 us  [on_device(): pl.pallas_call(kernel, out_shape=pltpu.VMEM((16, 16, CYCLES), f32), in_sp...]
where the time goes in v8:
time: 53.1 us; the launch traced here: 53 us
  Pallas kernels  52.3 us (98%)
  local copies, waits for them, and re-layouts  0.71 us (1%)
    pallas_call x1, Pallas kernels, on_device(): pl.pallas_call(kernel, out_shape=pltpu.VMEM((16, 16, CYCLES), f32), in_sp...  52.3 us

profile of v8, /device:TPU:1, one launch (start us, length us, event | category | flops | bytes accessed | tf_op | source)
XLA Modules:
  0.0 53.0 jit_solution(2209486230089188586)
XLA Ops:
  0.0 52.3 %kam.1 = f32[16,16,256]{2,1,0:T(8,128)S(1)} custom-call(bf16[16,256,1024]{2,1,0:T(8,128)(2,1)} %img_hbm.1, s32[128,256]{1,0:T(8,128)} %msk_hbm.1, f32[1,128]{1,0:T(1,128)} %bitcast.1, f32[128,128]{1,0:T(8,128)} %inv_hbm.1, bf16[256,1024]{1,0:T(8,128)(2,1)} %constant.2.clone.tab_hbm), custom_call_target="tpu_custom_call" | custom-call | tf_op jit(solution)/shard_map/kam/pallas_call | solution.py:272
  52.3 0.7 %copy.7 = f32[16,16,256]{2,1,0:T(8,128)} copy(f32[16,16,256]{2,1,0:T(8,128)S(1)} %kam.1) | data formatting | bytes 524288
